TPU v7x, 32 devices: a whole 2x2x4 slice. The times are simulated.
32 devices in a mesh: grp: 4 (over y, core), scen: 8 (over z, x).
Axes of the slice: x: 2, y: 2, z: 4, core: 2. Of those that a mesh axis runs over, the one named last changes fastest.
Arguments:
- linv: bfloat16 [64, 2048, 2048], P(('grp', 'scen'))
- link: bfloat16 [64, 2048, 512], P(('grp', 'scen')), may hold values from -0.125 to 0.125
- residual_rows: bfloat16 [64, 2048], P(('grp', 'scen')), may hold values from -24 to 24
- active: int32 [64], P(('grp', 'scen')), may hold values from 512 to 2048
- owner: int32 [64], P(('grp', 'scen')), may hold values from 0 to 63, each once
- weights: float32 [64], replicated, may hold values from 0.01 to 0.1
- first_diag: float32 [512], replicated, may hold values from 1 to 10
- first_rhs: float32 [512], replicated, may hold values from -24 to 24
Outputs:
- step_first: float32 [512], replicated
- scenario_newton_step: float32 [64, 2048], P(('grp', 'scen'))
All inputs are finite; a program needn't handle non-finite values.
Results may differ from a plain program's by a relative error of at most 0.0075.
Values sent between devices are 32-bit elements; how exact they have to be, the bound alone decides.
A program may use at most 128 MiB of HBM per device.

v0:
```python
import jax
import jax.numpy as jnp
from jax import lax
from jax.sharding import PartitionSpec as P

ITERS = 2


def body(linv, link, residual_rows, active, owner, weights, first_diag, first_rhs):
    local_count, rows = (linv.shape[0], linv.shape[1])
    width = link.shape[2]
    entry_offsets = lax.broadcasted_iota(jnp.int32, (local_count, rows), 1)
    keep = entry_offsets < active[:, None]
    masked = jnp.where(keep[:, :, None], link, jnp.zeros_like(link))
    solved = jnp.einsum("smk,skp->smp", linv, masked, preferred_element_type=jnp.float32).astype(
        jnp.bfloat16
    )
    lifted = jnp.einsum(
        "smk,sk->sm", linv, residual_rows, preferred_element_type=jnp.float32
    ).astype(jnp.bfloat16)
    numbers = lax.broadcasted_iota(jnp.int32, (local_count, weights.shape[0]), 1)
    probs = jnp.sum(jnp.where(owner[:, None] == numbers, weights[None, :], 0.0), axis=1)
    gram = jnp.einsum("smp,smq->spq", solved, solved, preferred_element_type=jnp.float32)
    cross = jnp.einsum("sm,smp->sp", lifted, solved, preferred_element_type=jnp.float32)
    partial_schur = jnp.einsum("s,spq->pq", probs, gram)
    partial_coupling_product = jnp.einsum("s,sp->p", probs, cross)
    grouped = (
        lax.psum_scatter(partial_schur, "scen", scatter_dimension=0, tiled=True),
        lax.psum_scatter(partial_coupling_product, "scen", scatter_dimension=0, tiled=True),
    )
    schur_share, cross_share = lax.psum((grouped[0], grouped[1]), "grp")
    offset = lax.axis_index("scen") * schur_share.shape[0]

    def collect(piece):
        return lax.all_gather(piece, "scen", axis=0, tiled=True)

    def totals(values):
        return lax.psum((values[0],), "scen")

    share_rows = schur_share.shape[0]
    row_ids = offset + lax.broadcasted_iota(jnp.int32, (share_rows, width), 0)
    col_ids = lax.broadcasted_iota(jnp.int32, (share_rows, width), 1)
    diag_rows = jnp.where(row_ids == col_ids, first_diag[None, :], 0.0)
    schur_rows = schur_share + diag_rows
    vector = lax.dynamic_slice_in_dim(first_rhs, offset, share_rows) - cross_share
    iterate = jnp.zeros_like(vector)
    remain = vector
    direction = vector
    norm_now = totals((jnp.sum(remain * remain),))[0]
    for step in range(ITERS):
        image = jnp.dot(schur_rows, collect(direction), precision=lax.Precision.HIGHEST)
        alpha = norm_now / totals((jnp.sum(direction * image),))[0]
        iterate = iterate + alpha * direction
        remain = remain - alpha * image
        norm_next = totals((jnp.sum(remain * remain),))[0]
        direction = remain + norm_next / norm_now * direction
        norm_now = norm_next
    step_first = collect(iterate)
    step_bf = step_first.astype(jnp.bfloat16)
    residue = lifted.astype(jnp.float32) - jnp.einsum(
        "smp,p->sm", solved, step_bf, preferred_element_type=jnp.float32
    )
    scenario_newton_step = jnp.einsum(
        "smk,sm->sk", linv, residue.astype(jnp.bfloat16), preferred_element_type=jnp.float32
    )
    return (step_first, scenario_newton_step)


def solution(mesh):
    placed = (
        P(("grp", "scen"), None, None),
        P(("grp", "scen"), None, None),
        P(("grp", "scen"), None),
        P(("grp", "scen")),
        P(("grp", "scen")),
        P(),
        P(),
        P(),
    )
    return jax.shard_map(
        body, mesh=mesh, in_specs=placed, out_specs=(P(), P(("grp", "scen"), None)), check_vma=False
    )
```

profile of v0, /device:TPU:0, one launch (start us, length us, event | category | flops | bytes accessed | tf_op | source)
XLA Modules:
  0.0 249.5 jit_solution(9905749967321219368)
XLA Ops:
  7.2 0.0 copy-start
  7.2 0.0 reduce-scatter.2.cloned.1.call-start
  7.2 0.7 iota_compare_fusion.1
  8.0 14.9 %fusion.5 = bf16[2,512,2048]{2,1,0:T(8,128)(2,1)S(1)} fusion(bf16[2,2048,2048]{2,1,0:T(8,128)(2,1)} %param.8, bf16[2,2048,512]{2,1,0:T(8,128)(2,1)} %param.9, pred[2,2048]{1,0:T(4,128)(4,1)S(1)} %iota_compare_fusion.1), kind=kOutput, calls=%fused_computation.5 | convolution fusion | flops 8594128896 | bytes 25169920 | tf_op jit(solution)/shard_map/smk,skp->smp/dot_general | solution.py:15
  22.9 0.0 copy-start.1
  22.9 0.0 copy-start.5
  22.9 0.0 copy-start.6
  22.9 2.4 fusion.38
  25.3 0.0 copy-done.1
  25.3 0.0 copy-done.5
  25.3 0.0 copy-done.6
  25.3 0.2 fusion.28
  25.5 1.2 fusion.9
  26.7 1.0 copy.43
  27.8 0.0 reduce-scatter.2.cloned.1.call-update
  27.8 0.2 all-reduce.7.cloned.1.call-start
  28.0 0.0 copy-done
  28.1 0.0 copy-start.3
  28.1 8.1 %fusion.24 = bf16[2,1,2048]{2,1,0:T(2,128)(2,1)S(1)} fusion(bf16[2,2048,2048]{2,1,0:T(8,128)(2,1)} %param.8, bf16[2,2048,1]{1,0,2:T(2,128)(2,1)S(1)} %bitcast.59), kind=kOutput, calls=%fused_computation.30 | convolution fusion | flops 16777216 | bytes 16793600 | tf_op jit(solution)/shard_map/smk,sk->sm/dot_general | solution.py:18
  36.1 0.0 copy-start.4
  36.2 0.0 copy-done.3
  36.2 0.6 fusion.37
  37.4 3.4 %fusion.22 = bf16[2,1,512]{2,1,0:T(2,128)(2,1)S(1)} fusion(bf16[2,512,2048]{2,1,0:T(8,128)(2,1)} %copy-done.1, bf16[2,2048,1]{1,0,2:T(2,128)(2,1)S(1)} %bitcast.61), kind=kOutput, calls=%fused_computation.28 | convolution fusion | flops 4194304 | bytes 4204544 | tf_op jit(solution)/shard_map/sm,smp->sp/dot_general | solution.py:24
  40.8 0.1 fusion.27
  40.9 23.2 %all-reduce.3 = f32[512]{0:T(512)S(1)} all-reduce(f32[512]{0:T(512)S(1)} %bitcast.65), channel_id=2, replica_groups=mesh['grp'=4,'scen'=8] {'scen'}, use_global_device_ids=true, to_apply=%region_1.2.clone | all-reduce | flops 512 | bytes 4096
  64.1 0.1 dynamic-slice.4
  64.8 5.7 %psum.42 = f32[64]{0:T(128)S(1)} all-reduce(f32[64]{0:T(128)S(1)} %dynamic-slice.4), channel_id=1, replica_groups=mesh['grp'=4,'scen'=8] {'grp'}, use_global_device_ids=true, to_apply=%region_2.3 | all-reduce | flops 64 | bytes 512 | tf_op jit(solution)/shard_map/psum | solution.py:31
  70.5 0.8 fusion.36
  71.3 17.3 %all-reduce = f32[512]{0:T(512)S(1)} all-reduce(f32[512]{0:T(512)S(1)} %get-tuple-element.8), channel_id=1, replica_groups=mesh['grp'=4,'scen'=8] {'scen'}, use_global_device_ids=true, to_apply=%add | all-reduce | flops 512 | bytes 4096
  88.7 5.4 %reduce-scatter.2.cloned.1.call-done = f32[64,512]{1,0:T(8,128)} async-done(((f32[512,512]{1,0:T(8,128)}), f32[64,512]{1,0:T(8,128)}) %reduce-scatter.2.cloned.1.call-update) | async-done | bytes 131088 | tf_op jit(solution)/shard_map/reduce_scatter | solution.py:28
  94.1 0.0 all-reduce.7.cloned.1.call-update
  94.1 32.8 %all-reduce.7.cloned.1.call-done = f32[64,512]{1,0:T(8,128)} async-done(((f32[64,512]{1,0:T(8,128)}), f32[64,512]{1,0:T(8,128)}) %all-reduce.7.cloned.1.call-update) | async-done | bytes 131088 | tf_op jit(solution)/shard_map/psum | solution.py:31
  126.9 0.0 copy-done.4
  126.9 1.8 multiply_reduce_fusion.1
  128.8 22.0 %all-reduce.4 = (f32[]{:T(128)}, f32[]{:T(128)}) all-reduce(f32[]{:T(128)} %get-tuple-element.3, f32[]{:T(128)} %get-tuple-element.2), channel_id=1, replica_groups=mesh['grp'=4,'scen'=8] {'scen'}, use_global_device_ids=true, to_apply=%region_4.5 | all-reduce | flops 2 | bytes 16 | tf_op jit(solution)/shard_map/psum | solution.py:38
  152.1 0.6 multiply_reduce_fusion
  152.7 17.7 %psum.46 = f32[]{:T(128)} all-reduce(f32[]{:T(128)} %multiply_reduce_fusion), channel_id=1, replica_groups=mesh['grp'=4,'scen'=8] {'scen'}, use_global_device_ids=true, to_apply=%region_10.11 | all-reduce | flops 1 | bytes 8 | tf_op jit(solution)/shard_map/psum | solution.py:38
  171.7 0.1 fusion.35
  171.8 19.1 %all-reduce.1 = f32[512]{0:T(512)S(1)} all-reduce(f32[512]{0:T(512)S(1)} %get-tuple-element.6), channel_id=1, replica_groups=mesh['grp'=4,'scen'=8] {'scen'}, use_global_device_ids=true, to_apply=%add.1 | all-reduce | flops 512 | bytes 4096
  191.0 1.8 fusion.12
  192.8 17.8 %psum.47 = f32[]{:T(128)} all-reduce(f32[]{:T(128)} %fusion.12), channel_id=1, replica_groups=mesh['grp'=4,'scen'=8] {'scen'}, use_global_device_ids=true, to_apply=%region_12.13 | all-reduce | flops 1 | bytes 8 | tf_op jit(solution)/shard_map/psum | solution.py:38
  211.9 0.1 add_dynamic-update-slice_fusion
  212.0 19.1 %all-reduce.2 = f32[512]{0:T(512)S(1)} all-reduce(f32[512]{0:T(512)S(1)} %add_dynamic-update-slice_fusion), channel_id=1, replica_groups=mesh['grp'=4,'scen'=8] {'scen'}, use_global_device_ids=true, to_apply=%add.2 | all-reduce | flops 512 | bytes 4096
  231.1 0.0 copy-start.2
  231.1 2.8 %fusion = f32[1,2,2048]{2,0,1:T(1,128)S(1)} fusion(bf16[512,1,1]{0,1,2:T(2,128)(2,1)S(1)} %reshape.53, bf16[2,512,2048]{2,1,0:T(8,128)(2,1)} %copy-done.1), kind=kOutput, calls=%fused_computation | convolution fusion | flops 4194304 | bytes 4211712 | tf_op jit(solution)/shard_map/smp,p->sm/dot_general | solution.py:60
  234.0 8.0 %fusion.20 = f32[2,1,2048]{2,1,0:T(1,128)S(1)} fusion(bf16[2,2048,2048]{2,1,0:T(8,128)(2,1)} %param.8, bf16[2,2048,1]{1,0,2:T(2,128)(2,1)S(1)} %fusion.26), kind=kOutput, calls=%fused_computation.26 | convolution fusion | flops 16777216 | bytes 16801792 | tf_op jit(solution)/shard_map/smk,sm->sk/dot_general | solution.py:63
  242.0 0.0 copy-done.2
  242.1 0.6 copy.44
  (8 shorter events, 0.0 us)
Async XLA Ops:
  7.2 20.9 %copy-start = (bf16[2,2048]{1,0:T(2,128)(2,1)S(1)}, bf16[2,2048]{1,0:T(2,128)(2,1)}, u32[]{:S(2)}) copy-start(bf16[2,2048]{1,0:T(2,128)(2,1)} %param.10) | copy-start | bytes 24580
  7.2 86.9 %reduce-scatter.2.cloned.1.call-start = ((), (), s32[]{:S(2)}) async-start(), calls=%async_computation.1 | async-start | bytes 1179648 | tf_op jit(solution)/shard_map/reduce_scatter | solution.py:28
  22.9 2.4 copy-start.1
  22.9 2.4 copy-start.5
  22.9 2.4 copy-start.6
  27.8 99.1 %all-reduce.7.cloned.1.call-start = ((), (), s32[]{:S(2)}) async-start(), calls=%async_computation.2 | async-start | bytes 262144 | tf_op jit(solution)/shard_map/psum | solution.py:31
  28.1 8.1 %copy-start.3 = (u32[32]{0:T(128)S(1)}, u32[32]{0:T(128)}, u32[]{:S(2)}) copy-start(u32[32]{0:T(128)} %constant.21) | copy-start | bytes 388
  36.1 90.8 %copy-start.4 = (f32[512]{0:T(512)S(1)}, f32[512]{0:T(512)}, u32[]{:S(2)}) copy-start(f32[512]{0:T(512)} %param.14) | copy-start | bytes 6148
  231.1 10.9 %copy-start.2 = (f32[512]{0:T(512)}, f32[512]{0:T(512)S(1)}, u32[]{:S(2)}) copy-start(f32[512]{0:T(512)S(1)} %all-reduce.2) | copy-start | bytes 6148
Sparse Core Ops, SparseCore 0:
  27.9 66.0 reduce-scatter.1
  96.5 30.3 all-reduce.6
where the time goes:
time: 250 us
  blocking collectives  142 us (57%)
  matrix products  44.6 us (18%)
  waiting for transfers between devices  38.3 us (15%)
  between operations  19.5 us (8%)
  other arithmetic  2.59 us (1%)
    unnamed x4, blocking collectives  78.7 us
    psum x3, blocking collectives, totals(): return lax.psum((values[0],), 'scen')  57.5 us
    psum x1, waiting for transfers between devices, body(): schur_share, cross_share = lax.psum((grouped[0], grouped[1]), 'grp')  32.8 us
    dot_general x1, matrix products, body(): jnp.einsum('smk,skp->smp', linv, masked, preferred_element_type=jnp.float32)  14.9 us
    dot_general x1, matrix products, body(): jnp.einsum('smk,sk->sm', linv, residual_rows, preferred_element_type=jnp....  8.05 us
    dot_general x1, matrix products, body(): jnp.einsum('smk,sm->sk', linv, residue.astype(jnp.bfloat16), preferred_el...  8.04 us
    psum x1, blocking collectives, body(): schur_share, cross_share = lax.psum((grouped[0], grouped[1]), 'grp')  5.67 us
    reduce_scatter x1, waiting for transfers between devices, body(): lax.psum_scatter(partial_schur, 'scen', scatter_dimension=0, tiled=True)  5.39 us
  transfers between devices with their start and end apart: 2, of which 2 were waited for; matrix products, arithmetic and copies ran while one was open for 5% of the time, Pallas kernels for 0%

commit v1 on v0

v1 whole, which is shorter than its diff:
```python
import functools
import math

import jax
import jax.numpy as jnp
from jax import lax
from jax.experimental import pallas as pl
from jax.experimental.pallas import tpu as pltpu
from jax.sharding import PartitionSpec as P

MESH = pl.DeviceIdType.MESH
NT = (((1,), (1,)), ((), ()))
BLOCK = 256
PAD = 16
LANES = 128
ROUNDS = 3
STAGES = (("grp",), ("scen",))


def member(axes, sizes, shift):
    me = 0
    for axis in axes:
        me = me * sizes[axis] + lax.axis_index(axis)
    other = lax.rem(me + shift, math.prod(sizes[axis] for axis in axes))
    place = {}
    for axis in reversed(axes):
        place[axis] = lax.rem(other, sizes[axis])
        other = lax.div(other, sizes[axis])
    return me, place


def split(row):
    high = row.astype(jnp.bfloat16).astype(jnp.float32)
    return high, row - high


def stack(rows):
    width = rows[0].shape[1]
    numbers = lax.broadcasted_iota(jnp.int32, (PAD, width), 0)
    out = jnp.zeros((PAD, width), jnp.float32)
    for number, row in enumerate(rows):
        out = jnp.where(numbers == number, row, out)
    return out.astype(jnp.bfloat16)


def to_tile(row, tile_rows):
    pieces = [row[:, at : at + LANES] for at in range(0, row.shape[1], LANES)]
    if len(pieces) < tile_rows:
        pieces.append(jnp.zeros((tile_rows - len(pieces), LANES), jnp.float32))
    return jnp.concatenate(pieces, axis=0)


def to_row(tile, width):
    return jnp.concatenate([tile[n : n + 1, :] for n in range(width // LANES)], axis=1)


def kernel(
    sizes,
    active_ref,
    owner_ref,
    weights_ref,
    residual_ref,
    diag_ref,
    rhs_ref,
    linv_hbm,
    link_hbm,
    step_ref,
    newton_ref,
    linv,
    link,
    lhs,
    solved,
    gram,
    back,
    *rest,
):
    count, rows, width = link.shape
    blocks = rows // BLOCK
    bufs = rest[: len(STAGES)]
    linv_sem, link_sem = rest[len(STAGES) : len(STAGES) + 2]
    send_sems = rest[len(STAGES) + 2 : 2 * len(STAGES) + 2]
    recv_sems = rest[2 * len(STAGES) + 2 :]
    tile_rows = bufs[0].shape[2]

    barrier = pltpu.get_barrier_semaphore()
    partners = 0
    for axes in STAGES:
        for shift in range(1, math.prod(sizes[axis] for axis in axes)):
            pl.semaphore_signal(
                barrier, inc=1, device_id=member(axes, sizes, shift)[1], device_id_type=MESH
            )
            partners += 1

    def linv_copy(s, i):
        part = (s, pl.ds(i * BLOCK, BLOCK), pl.ds(0, (i + 1) * BLOCK))
        return pltpu.make_async_copy(linv_hbm.at[part], linv.at[part], linv_sem.at[s, i])

    def link_copy(s, i):
        part = (s, pl.ds(i * BLOCK, BLOCK))
        return pltpu.make_async_copy(link_hbm.at[part], link.at[part], link_sem.at[s, i])

    for s in range(count):
        for i in range(blocks):
            link_copy(s, i).start()
            linv_copy(s, i).start()

    right = residual_ref[...].astype(jnp.float32)
    for s in range(count):
        lhs[s, width:, :] = stack([right[s : s + 1, :]])

    def turn(s, i):
        link_copy(s, i).wait()
        columns = link[s, i * BLOCK : (i + 1) * BLOCK, :].astype(jnp.float32)
        numbers = i * BLOCK + lax.broadcasted_iota(jnp.int32, (BLOCK, width), 0)
        masked = jnp.where(numbers < active_ref[s], columns, 0.0).astype(jnp.bfloat16)
        lhs[s, :width, i * BLOCK : (i + 1) * BLOCK] = masked.T

    def prepare(s, cross):
        turn(s, 0)
        for i in range(blocks):
            linv_copy(s, i).wait()
            if i + 1 < blocks:
                turn(s, i + 1)
            deep = (i + 1) * BLOCK
            out = lax.dot_general(
                lhs[s, :, :deep],
                linv[s, i * BLOCK : deep, :deep],
                NT,
                preferred_element_type=jnp.float32,
            )
            solved[s, :, i * BLOCK : deep] = out.astype(jnp.bfloat16)
        part = lax.dot_general(
            solved[s, width:, :], solved[s, :width, :], NT, preferred_element_type=jnp.float32
        )
        return cross + weights_ref[owner_ref[s]] * part[0:1, :]

    cross = lax.fori_loop(0, count, prepare, jnp.zeros((1, width), jnp.float32))
    pl.semaphore_wait(barrier, partners)

    def total(turn_number, tile, beside):
        for stage, axes in enumerate(STAGES):
            buf = bufs[stage]
            n = buf.shape[1]
            me = member(axes, sizes, 0)[0]
            buf[turn_number, me] = tile
            copies = []
            for shift in range(1, n):
                copies.append(
                    pltpu.make_async_remote_copy(
                        src_ref=buf.at[turn_number, me],
                        dst_ref=buf.at[turn_number, me],
                        send_sem=send_sems[stage].at[turn_number, shift],
                        recv_sem=recv_sems[stage].at[turn_number, shift],
                        device_id=member(axes, sizes, shift)[1],
                        device_id_type=MESH,
                    )
                )
                copies[-1].start()
            for s in range(count):
                if s * len(STAGES) // count == stage:
                    beside(s)
            for copy in copies:
                copy.wait()
            tile = buf[turn_number, 0]
            for number in range(1, n):
                tile = tile + buf[turn_number, number]
        return tile

    def add_gram(s):
        part = lax.dot_general(
            solved[s, :width, :], solved[s, :width, :], NT, preferred_element_type=jnp.float32
        )
        part = weights_ref[owner_ref[s]] * part
        gram[...] = part if s == 0 else gram[...] + part

    def times_gram(row):
        spread = jnp.broadcast_to(row, (8, width))
        out = jnp.dot(
            spread, gram[...], precision=lax.Precision.HIGHEST, preferred_element_type=jnp.float32
        )
        return out[0:1, :]

    def dots(left, other):
        return jnp.sum(left * other, axis=1, keepdims=True)

    diag = diag_ref[...]
    vector = rhs_ref[...] - to_row(total(0, to_tile(cross, tile_rows), add_gram), width)
    norm_first = dots(vector, vector)
    summed = total(1, to_tile(times_gram(vector), tile_rows), lambda s: None)
    image = diag * vector + to_row(summed, width)
    alpha = norm_first / dots(vector, image)
    iterate = alpha * vector
    remain = vector - alpha * image
    norm_next = dots(remain, remain)
    direction = remain + (norm_next / norm_first) * vector
    local = dots(direction, times_gram(direction))
    both = stack([*split(iterate), *split(direction)])

    def back_solve(s):
        taken = jnp.dot(both, solved[s, :width, :], preferred_element_type=jnp.float32)
        lifted = solved[s, width:, :].astype(jnp.float32)[0:1, :]
        residue = lifted - (taken[0:1, :] + taken[1:2, :])
        slope = taken[2:3, :] + taken[3:4, :]
        sides = stack([*split(residue), *split(slope)])
        for j in range(blocks):
            back[s, :, j * BLOCK : (j + 1) * BLOCK] = jnp.dot(
                sides[:, j * BLOCK :],
                linv[s, j * BLOCK :, j * BLOCK : (j + 1) * BLOCK],
                preferred_element_type=jnp.float32,
            )

    curved = total(2, jnp.broadcast_to(local, (tile_rows, LANES)), back_solve)[0:1, 0:1]
    alpha = norm_next / (dots(direction, diag * direction) + curved)
    step_ref[...] = iterate + alpha * direction
    for s in range(count):
        newton_ref[s : s + 1, :] = (back[s, 0:1, :] + back[s, 1:2, :]) - alpha * (
            back[s, 2:3, :] + back[s, 3:4, :]
        )


def body(sizes, linv, link, residual_rows, active, owner, weights, first_diag, first_rhs):
    count, rows, width = link.shape
    blocks = rows // BLOCK
    tile_rows = -(-width // (8 * LANES)) * 8
    members = [math.prod(sizes[axis] for axis in axes) for axes in STAGES]
    smem = pl.BlockSpec(memory_space=pltpu.SMEM)
    vmem = pl.BlockSpec(memory_space=pltpu.VMEM)
    hbm = pl.BlockSpec(memory_space=pl.ANY)
    step, newton = pl.pallas_call(
        functools.partial(kernel, sizes),
        out_shape=(
            jax.ShapeDtypeStruct((1, width), jnp.float32),
            jax.ShapeDtypeStruct((count, rows), jnp.float32),
        ),
        in_specs=[smem, smem, smem, vmem, vmem, vmem, hbm, hbm],
        out_specs=(vmem, vmem),
        scratch_shapes=[
            pltpu.VMEM((count, rows, rows), jnp.bfloat16),
            pltpu.VMEM((count, rows, width), jnp.bfloat16),
            pltpu.VMEM((count, width + PAD, rows), jnp.bfloat16),
            pltpu.VMEM((count, width + PAD, rows), jnp.bfloat16),
            pltpu.VMEM((width, width), jnp.float32),
            pltpu.VMEM((count, PAD, rows), jnp.float32),
            *[pltpu.VMEM((ROUNDS, n, tile_rows, LANES), jnp.float32) for n in members],
            pltpu.SemaphoreType.DMA((count, blocks)),
            pltpu.SemaphoreType.DMA((count, blocks)),
            *[pltpu.SemaphoreType.DMA((ROUNDS, n)) for n in members],
            *[pltpu.SemaphoreType.DMA((ROUNDS, n)) for n in members],
        ],
        compiler_params=pltpu.CompilerParams(
            collective_id=0, has_side_effects=True, vmem_limit_bytes=56 * 1024 * 1024
        ),
    )(
        active,
        owner,
        weights,
        residual_rows,
        first_diag.reshape(1, width),
        first_rhs.reshape(1, width),
        linv,
        link,
    )
    return step.reshape(width), newton


def solution(mesh):
    shared = ("grp", "scen")
    placed = (
        P(shared, None, None),
        P(shared, None, None),
        P(shared, None),
        P(shared),
        P(shared),
        P(),
        P(),
        P(),
    )
    return jax.shard_map(
        functools.partial(body, dict(mesh.shape)),
        mesh=mesh,
        in_specs=placed,
        out_specs=(P(), P(shared, None)),
        check_vma=False,
    )
```

time: 250 us -> 47 us (0.19)
  blocking collectives: 142 us -> 0 us
  matrix products: 44.6 us -> 0 us
  Pallas kernels: 0 us -> 43.5 us
  waiting for transfers between devices: 38.3 us -> 0 us
  between operations: 19.5 us -> 0.64 us
  other arithmetic: 2.59 us -> 0 us
    unnamed x4 -> x0, blocking collectives: 78.7 us -> none
    psum x4 -> x0, blocking collectives: 63.2 us -> none  [the longest x3 57.5 us: totals(): return lax.psum((values[0],), 'scen')]
    dot_general x10 -> x0, matrix products: 44.6 us -> none  [the longest x1 14.9 us: body(): jnp.einsum('smk,skp->smp', linv, masked, preferred_element_type=jnp.float32)]
    pallas_call x0 -> x1, Pallas kernels: none -> 43.5 us  [body(): pl.pallas_call(functools.partial(kernel, sizes), out_shape=(jax.ShapeDtyp...]
    psum x1 -> x0, waiting for transfers between devices: 32.8 us -> none  [body(): schur_share, cross_share = lax.psum((grouped[0], grouped[1]), 'grp')]
    reduce_scatter x1 -> x0, waiting for transfers between devices: 5.39 us -> none  [body(): lax.psum_scatter(partial_schur, 'scen', scatter_dimension=0, tiled=True)]
  transfers between devices with their start and end apart: 2 -> 0, of which waited for: 2 -> 0; matrix products, arithmetic and copies ran while one was open for 5% -> 0% of each run, Pallas kernels for 0% -> 0%
where the time goes in v1:
time: 47 us; the launch traced here: 46.7 us
  Pallas kernels  43.5 us (93%)
  local copies, waits for them, and re-layouts  2.55 us (5%)
  between operations  0.64 us (1%)
    pallas_call x1, Pallas kernels, body(): pl.pallas_call(functools.partial(kernel, sizes), out_shape=(jax.ShapeDtyp...  43.5 us
    unnamed x2, local copies, waits for them, and re-layouts  2.55 us

profile of v1, /device:TPU:0, one launch (start us, length us, event | category | flops | bytes accessed | tf_op | source)
XLA Modules:
  0.0 46.7 jit_solution(653873059391752662)
XLA Ops:
  0.6 43.5 %shard_map.95 = (f32[1,512]{1,0:T(1,128)}, f32[2,2048]{1,0:T(2,128)}) custom-call(s32[2]{0:T(128)} %active_ref.1, s32[2]{0:T(128)} %owner_ref.1, f32[64]{0:T(128)} %weights_ref.1, bf16[2,2048]{1,0:T(2,128)(2,1)} %residual_ref.1, f32[1,512]{1,0:T(1,128)} %bitcast.3, f32[1,512]{1,0:T(1,128)} %bitcast.4, bf16[2,2048,2048]{2,1,0:T(8,128)(2,1)} %linv_hbm.1, ...), custom_call_target="tpu_custom_call" | custom-call | tf_op jit(solution)/shard_map/pallas_call | solution.py:229
  44.1 1.2 %copy.12 = f32[512]{0:T(512)} copy(f32[512]{0:T(512)} %bitcast.5) | data formatting | bytes 4096
  45.4 1.3 %copy.13 = f32[2,2048]{1,0:T(2,128)} copy(f32[2,2048]{1,0:T(2,128)} %get-tuple-element.9) | data formatting | bytes 32768

commit v2 on v1

--- a/solution.py
+++ b/solution.py
@@ -11,6 +11,7 @@
 MESH = pl.DeviceIdType.MESH
 NT = (((1,), (1,)), ((), ()))
 BLOCK = 256
+GROUP = 2
 PAD = 16
 LANES = 128
 ROUNDS = 3
@@ -43,11 +44,10 @@
     return out.astype(jnp.bfloat16)
 
 
-def to_tile(row, tile_rows):
-    pieces = [row[:, at : at + LANES] for at in range(0, row.shape[1], LANES)]
-    if len(pieces) < tile_rows:
-        pieces.append(jnp.zeros((tile_rows - len(pieces), LANES), jnp.float32))
-    return jnp.concatenate(pieces, axis=0)
+def to_tile(row):
+    return jnp.concatenate(
+        [row[:, at : at + LANES] for at in range(0, row.shape[1], LANES)], axis=0
+    )
 
 
 def to_row(tile, width):
@@ -80,7 +80,19 @@
     linv_sem, link_sem = rest[len(STAGES) : len(STAGES) + 2]
     send_sems = rest[len(STAGES) + 2 : 2 * len(STAGES) + 2]
     recv_sems = rest[2 * len(STAGES) + 2 :]
-    tile_rows = bufs[0].shape[2]
+
+    def linv_copy(s, i):
+        part = (s, pl.ds(i * BLOCK, BLOCK), pl.ds(0, (i + 1) * BLOCK))
+        return pltpu.make_async_copy(linv_hbm.at[part], linv.at[part], linv_sem.at[s, i])
+
+    def link_copy(s, i):
+        part = (s, pl.ds(i * BLOCK, BLOCK))
+        return pltpu.make_async_copy(link_hbm.at[part], link.at[part], link_sem.at[s, i])
+
+    for s in range(count):
+        for i in range(blocks):
+            link_copy(s, i).start()
+            linv_copy(s, i).start()
 
     barrier = pltpu.get_barrier_semaphore()
     partners = 0
@@ -91,50 +103,54 @@
             )
             partners += 1
 
-    def linv_copy(s, i):
-        part = (s, pl.ds(i * BLOCK, BLOCK), pl.ds(0, (i + 1) * BLOCK))
-        return pltpu.make_async_copy(linv_hbm.at[part], linv.at[part], linv_sem.at[s, i])
-
-    def link_copy(s, i):
-        part = (s, pl.ds(i * BLOCK, BLOCK))
-        return pltpu.make_async_copy(link_hbm.at[part], link.at[part], link_sem.at[s, i])
-
-    for s in range(count):
-        for i in range(blocks):
-            link_copy(s, i).start()
-            linv_copy(s, i).start()
-
     right = residual_ref[...].astype(jnp.float32)
     for s in range(count):
         lhs[s, width:, :] = stack([right[s : s + 1, :]])
 
     def turn(s, i):
-        link_copy(s, i).wait()
         columns = link[s, i * BLOCK : (i + 1) * BLOCK, :].astype(jnp.float32)
         numbers = i * BLOCK + lax.broadcasted_iota(jnp.int32, (BLOCK, width), 0)
         masked = jnp.where(numbers < active_ref[s], columns, 0.0).astype(jnp.bfloat16)
         lhs[s, :width, i * BLOCK : (i + 1) * BLOCK] = masked.T
 
-    def prepare(s, cross):
-        turn(s, 0)
-        for i in range(blocks):
+    def solve(s, i):
+        deep = (i + 1) * BLOCK
+        out = lax.dot_general(
+            lhs[s, :, :deep],
+            linv[s, i * BLOCK : deep, :deep],
+            NT,
+            preferred_element_type=jnp.float32,
+        )
+        solved[s, :, i * BLOCK : deep] = out.astype(jnp.bfloat16)
+
+    steps = [
+        [(s, i) for i in range(at, min(at + GROUP, blocks))]
+        for s in range(count)
+        for at in range(0, blocks, GROUP)
+    ]
+    for s, i in steps[0]:
+        link_copy(s, i).wait()
+        turn(s, i)
+    cross = jnp.zeros((1, width), jnp.float32)
+    for number, step in enumerate(steps):
+        later = steps[number + 1] if number + 1 < len(steps) else []
+        for s, i in step:
             linv_copy(s, i).wait()
-            if i + 1 < blocks:
-                turn(s, i + 1)
-            deep = (i + 1) * BLOCK
-            out = lax.dot_general(
-                lhs[s, :, :deep],
-                linv[s, i * BLOCK : deep, :deep],
+        for s, i in later:
+            link_copy(s, i).wait()
+        for s, i in later:
+            turn(s, i)
+        for s, i in step:
+            solve(s, i)
+        part = jnp.zeros((PAD, width), jnp.float32)
+        for s, i in step:
+            part = part + lax.dot_general(
+                solved[s, width:, i * BLOCK : (i + 1) * BLOCK],
+                solved[s, :width, i * BLOCK : (i + 1) * BLOCK],
                 NT,
                 preferred_element_type=jnp.float32,
             )
-            solved[s, :, i * BLOCK : deep] = out.astype(jnp.bfloat16)
-        part = lax.dot_general(
-            solved[s, width:, :], solved[s, :width, :], NT, preferred_element_type=jnp.float32
-        )
-        return cross + weights_ref[owner_ref[s]] * part[0:1, :]
-
-    cross = lax.fori_loop(0, count, prepare, jnp.zeros((1, width), jnp.float32))
+        cross = cross + weights_ref[owner_ref[step[0][0]]] * part[0:1, :]
     pl.semaphore_wait(barrier, partners)
 
     def total(turn_number, tile, beside):
@@ -142,13 +158,14 @@
             buf = bufs[stage]
             n = buf.shape[1]
             me = member(axes, sizes, 0)[0]
-            buf[turn_number, me] = tile
+            sent = pl.ds(0, tile.shape[0])
+            buf[turn_number, me, sent] = tile
             copies = []
             for shift in range(1, n):
                 copies.append(
                     pltpu.make_async_remote_copy(
-                        src_ref=buf.at[turn_number, me],
-                        dst_ref=buf.at[turn_number, me],
+                        src_ref=buf.at[turn_number, me, sent],
+                        dst_ref=buf.at[turn_number, me, sent],
                         send_sem=send_sems[stage].at[turn_number, shift],
                         recv_sem=recv_sems[stage].at[turn_number, shift],
                         device_id=member(axes, sizes, shift)[1],
@@ -161,9 +178,9 @@
                     beside(s)
             for copy in copies:
                 copy.wait()
-            tile = buf[turn_number, 0]
+            tile = buf[turn_number, 0, sent]
             for number in range(1, n):
-                tile = tile + buf[turn_number, number]
+                tile = tile + buf[turn_number, number, sent]
         return tile
 
     def add_gram(s):
@@ -174,19 +191,23 @@
         gram[...] = part if s == 0 else gram[...] + part
 
     def times_gram(row):
-        spread = jnp.broadcast_to(row, (8, width))
-        out = jnp.dot(
-            spread, gram[...], precision=lax.Precision.HIGHEST, preferred_element_type=jnp.float32
-        )
+        part = gram[:, :LANES] * row[:, :LANES]
+        for at in range(LANES, width, LANES):
+            part = part + gram[:, at : at + LANES] * row[:, at : at + LANES]
+        high, rest_high = split(part)
+        middle, low = split(rest_high)
+        parts = jnp.concatenate([high, middle, low], axis=1).astype(jnp.bfloat16)
+        ones = jnp.ones((PAD, 3 * LANES), jnp.bfloat16)
+        out = lax.dot_general(ones, parts, NT, preferred_element_type=jnp.float32)
         return out[0:1, :]
 
     def dots(left, other):
         return jnp.sum(left * other, axis=1, keepdims=True)
 
     diag = diag_ref[...]
-    vector = rhs_ref[...] - to_row(total(0, to_tile(cross, tile_rows), add_gram), width)
+    vector = rhs_ref[...] - to_row(total(0, to_tile(cross), add_gram), width)
     norm_first = dots(vector, vector)
-    summed = total(1, to_tile(times_gram(vector), tile_rows), lambda s: None)
+    summed = total(1, to_tile(times_gram(vector)), lambda s: None)
     image = diag * vector + to_row(summed, width)
     alpha = norm_first / dots(vector, image)
     iterate = alpha * vector
@@ -209,13 +230,18 @@
                 preferred_element_type=jnp.float32,
             )
 
-    curved = total(2, jnp.broadcast_to(local, (tile_rows, LANES)), back_solve)[0:1, 0:1]
+    curved = total(2, jnp.broadcast_to(local, (1, LANES)), back_solve)[0:1, 0:1]
     alpha = norm_next / (dots(direction, diag * direction) + curved)
     step_ref[...] = iterate + alpha * direction
     for s in range(count):
         newton_ref[s : s + 1, :] = (back[s, 0:1, :] + back[s, 1:2, :]) - alpha * (
             back[s, 2:3, :] + back[s, 3:4, :]
         )
+
+
+def finish(step_ref, newton_ref, step_out, newton_out):
+    step_out[...] = step_ref[...]
+    newton_out[...] = newton_ref[...]
 
 
 def body(sizes, linv, link, residual_rows, active, owner, weights, first_diag, first_rhs):
@@ -226,12 +252,13 @@
     smem = pl.BlockSpec(memory_space=pltpu.SMEM)
     vmem = pl.BlockSpec(memory_space=pltpu.VMEM)
     hbm = pl.BlockSpec(memory_space=pl.ANY)
-    step, newton = pl.pallas_call(
+    shapes = (
+        jax.ShapeDtypeStruct((1, width), jnp.float32),
+        jax.ShapeDtypeStruct((count, rows), jnp.float32),
+    )
+    made = pl.pallas_call(
         functools.partial(kernel, sizes),
-        out_shape=(
-            jax.ShapeDtypeStruct((1, width), jnp.float32),
-            jax.ShapeDtypeStruct((count, rows), jnp.float32),
-        ),
+        out_shape=tuple(pltpu.VMEM(shape.shape, shape.dtype) for shape in shapes),
         in_specs=[smem, smem, smem, vmem, vmem, vmem, hbm, hbm],
         out_specs=(vmem, vmem),
         scratch_shapes=[
@@ -260,6 +287,9 @@
         linv,
         link,
     )
+    step, newton = pl.pallas_call(
+        finish, out_shape=shapes, in_specs=[vmem, vmem], out_specs=(vmem, vmem)
+    )(*made)
     return step.reshape(width), newton
 
 

time: 47 us -> 43.2 us (0.919)
  Pallas kernels: 43.5 us -> 41.2 us
  local copies, waits for them, and re-layouts: 2.55 us -> 1.16 us
    pallas_call x1 -> x2, Pallas kernels: 43.5 us -> 41.2 us  [the longest x1 39.8 us: body(): pl.pallas_call(functools.partial(kernel, sizes), out_shape=tuple((pltpu.V...]
    unnamed x2 -> x4, local copies, waits for them, and re-layouts: 2.55 us -> 1.16 us
where the time goes in v2:
time: 43.2 us; the launch traced here: 43 us
  Pallas kernels  41.2 us (95%)
  local copies, waits for them, and re-layouts  1.16 us (3%)
  between operations  0.65 us (2%)
    pallas_call x1, Pallas kernels, body(): pl.pallas_call(functools.partial(kernel, sizes), out_shape=tuple((pltpu.V...  39.8 us
    pallas_call x1, Pallas kernels, body(): pl.pallas_call(finish, out_shape=shapes, in_specs=[vmem, vmem], out_specs...  1.33 us
    unnamed x4, local copies, waits for them, and re-layouts  1.16 us

profile of v2, /device:TPU:0, one launch (start us, length us, event | category | flops | bytes accessed | tf_op | source)
XLA Modules:
  0.0 43.0 jit_solution(5697096106522542091)
XLA Ops:
  0.6 39.8 %shard_map.95 = (f32[1,512]{1,0:T(1,128)S(1)}, f32[2,2048]{1,0:T(2,128)S(1)}) custom-call(s32[2]{0:T(128)} %active_ref.1, s32[2]{0:T(128)} %owner_ref.1, f32[64]{0:T(128)} %weights_ref.1, bf16[2,2048]{1,0:T(2,128)(2,1)} %residual_ref.1, f32[1,512]{1,0:T(1,128)} %bitcast.3, f32[1,512]{1,0:T(1,128)} %bitcast.4, bf16[2,2048,2048]{2,1,0:T(8,128)(2,1)} %linv_hbm.1, ...), custom_call_target="tpu_custom_call" | custom-call | tf_op jit(solution)/shard_map/pallas_call | solution.py:259
  40.5 0.0 copy-start
  40.5 0.6 %copy-done = f32[2,2048]{1,0:T(2,128)} copy-done((f32[2,2048]{1,0:T(2,128)}, f32[2,2048]{1,0:T(2,128)S(1)}, u32[]{:S(2)}) %copy-start) | copy-done | bytes 16408
  41.1 0.0 copy-start.1
  41.1 0.6 %copy-done.1 = f32[1,512]{1,0:T(1,128)} copy-done((f32[1,512]{1,0:T(1,128)}, f32[1,512]{1,0:T(1,128)S(1)}, u32[]{:S(2)}) %copy-start.1) | copy-done | bytes 2072
  41.7 1.3 %shard_map.96 = (f32[1,512]{1,0:T(1,128)}, f32[2,2048]{1,0:T(2,128)}) custom-call(f32[1,512]{1,0:T(1,128)} %copy-done.1, f32[2,2048]{1,0:T(2,128)} %copy-done), custom_call_target="tpu_custom_call" | custom-call | tf_op jit(solution)/shard_map/pallas_call | solution.py:290
Async XLA Ops:
  40.5 0.6 %copy-start = (f32[2,2048]{1,0:T(2,128)}, f32[2,2048]{1,0:T(2,128)S(1)}, u32[]{:S(2)}) copy-start(f32[2,2048]{1,0:T(2,128)S(1)} %get-tuple-element.7.newton_ref) | copy-start | bytes 49156
  41.1 0.6 %copy-start.1 = (f32[1,512]{1,0:T(1,128)}, f32[1,512]{1,0:T(1,128)S(1)}, u32[]{:S(2)}) copy-start(f32[1,512]{1,0:T(1,128)S(1)} %get-tuple-element.6.step_ref) | copy-start | bytes 6148

commit v3 on v2

--- a/solution.py
+++ b/solution.py
@@ -11,7 +11,7 @@
 MESH = pl.DeviceIdType.MESH
 NT = (((1,), (1,)), ((), ()))
 BLOCK = 256
-GROUP = 2
+TAIL = 2
 PAD = 16
 LANES = 128
 ROUNDS = 3
@@ -72,6 +72,13 @@
     solved,
     gram,
     back,
+    active,
+    owner,
+    weights,
+    residual,
+    first_diag,
+    first_rhs,
+    small_sem,
     *rest,
 ):
     count, rows, width = link.shape
@@ -89,8 +96,26 @@
         part = (s, pl.ds(i * BLOCK, BLOCK))
         return pltpu.make_async_copy(link_hbm.at[part], link.at[part], link_sem.at[s, i])
 
+    small = [
+        pltpu.make_async_copy(source, target, small_sem.at[number])
+        for number, (source, target) in enumerate(
+            (
+                (active_ref, active),
+                (residual_ref, residual),
+                (owner_ref, owner),
+                (weights_ref, weights),
+                (diag_ref, first_diag),
+                (rhs_ref, first_rhs),
+            )
+        )
+    ]
+    for copy in small[:2]:
+        copy.start()
     for s in range(count):
         for i in range(blocks):
+            if s == 0 and i == 1:
+                for copy in small[2:]:
+                    copy.start()
             link_copy(s, i).start()
             linv_copy(s, i).start()
 
@@ -103,14 +128,16 @@
             )
             partners += 1
 
-    right = residual_ref[...].astype(jnp.float32)
+    for copy in small:
+        copy.wait()
+    right = residual[...].astype(jnp.float32)
     for s in range(count):
         lhs[s, width:, :] = stack([right[s : s + 1, :]])
 
     def turn(s, i):
         columns = link[s, i * BLOCK : (i + 1) * BLOCK, :].astype(jnp.float32)
         numbers = i * BLOCK + lax.broadcasted_iota(jnp.int32, (BLOCK, width), 0)
-        masked = jnp.where(numbers < active_ref[s], columns, 0.0).astype(jnp.bfloat16)
+        masked = jnp.where(numbers < active[s], columns, 0.0).astype(jnp.bfloat16)
         lhs[s, :width, i * BLOCK : (i + 1) * BLOCK] = masked.T
 
     def solve(s, i):
@@ -123,11 +150,22 @@
         )
         solved[s, :, i * BLOCK : deep] = out.astype(jnp.bfloat16)
 
-    steps = [
-        [(s, i) for i in range(at, min(at + GROUP, blocks))]
-        for s in range(count)
-        for at in range(0, blocks, GROUP)
-    ]
+    steps = []
+    for s in range(count):
+        cuts = {0, blocks, max(blocks - TAIL, 0)} if s else {0, TAIL, 2 * TAIL, blocks}
+        cuts = sorted(cut for cut in cuts if cut <= blocks)
+        steps += [[(s, i) for i in range(*pair)] for pair in zip(cuts, cuts[1:])]
+
+    def crossed(step):
+        s, low, high = step[0][0], step[0][1] * BLOCK, (step[-1][1] + 1) * BLOCK
+        part = lax.dot_general(
+            solved[s, width:, low:high],
+            solved[s, :width, low:high],
+            NT,
+            preferred_element_type=jnp.float32,
+        )
+        return weights[owner[s]] * part[0:1, :]
+
     for s, i in steps[0]:
         link_copy(s, i).wait()
         turn(s, i)
@@ -142,16 +180,12 @@
             turn(s, i)
         for s, i in step:
             solve(s, i)
-        part = jnp.zeros((PAD, width), jnp.float32)
-        for s, i in step:
-            part = part + lax.dot_general(
-                solved[s, width:, i * BLOCK : (i + 1) * BLOCK],
-                solved[s, :width, i * BLOCK : (i + 1) * BLOCK],
-                NT,
-                preferred_element_type=jnp.float32,
-            )
-        cross = cross + weights_ref[owner_ref[step[0][0]]] * part[0:1, :]
+        if number:
+            cross = cross + crossed(steps[number - 1])
+    cross = cross + crossed(steps[-1])
     pl.semaphore_wait(barrier, partners)
+
+    sends = []
 
     def total(turn_number, tile, beside):
         for stage, axes in enumerate(STAGES):
@@ -177,7 +211,8 @@
                 if s * len(STAGES) // count == stage:
                     beside(s)
             for copy in copies:
-                copy.wait()
+                copy.wait_recv()
+            sends.extend(copies)
             tile = buf[turn_number, 0, sent]
             for number in range(1, n):
                 tile = tile + buf[turn_number, number, sent]
@@ -187,7 +222,7 @@
         part = lax.dot_general(
             solved[s, :width, :], solved[s, :width, :], NT, preferred_element_type=jnp.float32
         )
-        part = weights_ref[owner_ref[s]] * part
+        part = weights[owner[s]] * part
         gram[...] = part if s == 0 else gram[...] + part
 
     def times_gram(row):
@@ -204,8 +239,8 @@
     def dots(left, other):
         return jnp.sum(left * other, axis=1, keepdims=True)
 
-    diag = diag_ref[...]
-    vector = rhs_ref[...] - to_row(total(0, to_tile(cross), add_gram), width)
+    diag = first_diag[...]
+    vector = first_rhs[...] - to_row(total(0, to_tile(cross), add_gram), width)
     norm_first = dots(vector, vector)
     summed = total(1, to_tile(times_gram(vector)), lambda s: None)
     image = diag * vector + to_row(summed, width)
@@ -237,6 +272,8 @@
         newton_ref[s : s + 1, :] = (back[s, 0:1, :] + back[s, 1:2, :]) - alpha * (
             back[s, 2:3, :] + back[s, 3:4, :]
         )
+    for copy in sends:
+        copy.wait_send()
 
 
 def finish(step_ref, newton_ref, step_out, newton_out):
@@ -249,7 +286,6 @@
     blocks = rows // BLOCK
     tile_rows = -(-width // (8 * LANES)) * 8
     members = [math.prod(sizes[axis] for axis in axes) for axes in STAGES]
-    smem = pl.BlockSpec(memory_space=pltpu.SMEM)
     vmem = pl.BlockSpec(memory_space=pltpu.VMEM)
     hbm = pl.BlockSpec(memory_space=pl.ANY)
     shapes = (
@@ -259,7 +295,7 @@
     made = pl.pallas_call(
         functools.partial(kernel, sizes),
         out_shape=tuple(pltpu.VMEM(shape.shape, shape.dtype) for shape in shapes),
-        in_specs=[smem, smem, smem, vmem, vmem, vmem, hbm, hbm],
+        in_specs=[hbm] * 8,
         out_specs=(vmem, vmem),
         scratch_shapes=[
             pltpu.VMEM((count, rows, rows), jnp.bfloat16),
@@ -268,6 +304,13 @@
             pltpu.VMEM((count, width + PAD, rows), jnp.bfloat16),
             pltpu.VMEM((width, width), jnp.float32),
             pltpu.VMEM((count, PAD, rows), jnp.float32),
+            pltpu.SMEM(active.shape, active.dtype),
+            pltpu.SMEM(owner.shape, owner.dtype),
+            pltpu.SMEM(weights.shape, weights.dtype),
+            pltpu.VMEM(residual_rows.shape, residual_rows.dtype),
+            pltpu.VMEM((1, width), jnp.float32),
+            pltpu.VMEM((1, width), jnp.float32),
+            pltpu.SemaphoreType.DMA((6,)),
             *[pltpu.VMEM((ROUNDS, n, tile_rows, LANES), jnp.float32) for n in members],
             pltpu.SemaphoreType.DMA((count, blocks)),
             pltpu.SemaphoreType.DMA((count, blocks)),
@@ -288,7 +331,11 @@
         link,
     )
     step, newton = pl.pallas_call(
-        finish, out_shape=shapes, in_specs=[vmem, vmem], out_specs=(vmem, vmem)
+        finish,
+        out_shape=shapes,
+        in_specs=[vmem, vmem],
+        out_specs=(vmem, vmem),
+        compiler_params=pltpu.CompilerParams(vmem_limit_bytes=1024 * 1024),
     )(*made)
     return step.reshape(width), newton
 

time: 43.2 us -> 41.4 us (0.958)
  local copies, waits for them, and re-layouts: 1.16 us -> 0 us
  Pallas kernels: 41.2 us -> 40.6 us
    unnamed x4 -> x0, local copies, waits for them, and re-layouts: 1.16 us -> none
    pallas_call x1, Pallas kernels: 1.33 us -> 0.61 us  [body(): pl.pallas_call(finish, out_shape=shapes, in_specs=[vmem, vmem], out_specs...]
where the time goes in v3:
time: 41.4 us; the launch traced here: 41.3 us
  Pallas kernels  40.6 us (98%)
  between operations  0.64 us (2%)
    pallas_call x1, Pallas kernels, body(): pl.pallas_call(functools.partial(kernel, sizes), out_shape=tuple((pltpu.V...  40 us

profile of v3, /device:TPU:0, one launch (start us, length us, event | category | flops | bytes accessed | tf_op | source)
XLA Modules:
  0.0 41.3 jit_solution(12003450275096486752)
XLA Ops:
  0.6 40.0 %shard_map.95 = (f32[1,512]{1,0:T(1,128)S(1)}, f32[2,2048]{1,0:T(2,128)S(1)}) custom-call(s32[2]{0:T(128)} %active_ref.1, s32[2]{0:T(128)} %owner_ref.1, f32[64]{0:T(128)} %weights_ref.1, bf16[2,2048]{1,0:T(2,128)(2,1)} %residual_ref.1, f32[1,512]{1,0:T(1,128)} %bitcast.3, f32[1,512]{1,0:T(1,128)} %bitcast.4, bf16[2,2048,2048]{2,1,0:T(8,128)(2,1)} %linv_hbm.1, ...), custom_call_target="tpu_custom_call" | custom-call | tf_op jit(solution)/shard_map/pallas_call | solution.py:295
  40.7 0.6 %shard_map.96 = (f32[1,512]{1,0:T(1,128)}, f32[2,2048]{1,0:T(2,128)}) custom-call(f32[1,512]{1,0:T(1,128)S(1)} %get-tuple-element.6.step_ref, f32[2,2048]{1,0:T(2,128)S(1)} %get-tuple-element.7.newton_ref), custom_call_target="tpu_custom_call" | custom-call | tf_op jit(solution)/shard_map/pallas_call | solution.py:333

commit v4 on v3

--- a/solution.py
+++ b/solution.py
@@ -219,11 +219,18 @@
         return tile
 
     def add_gram(s):
-        part = lax.dot_general(
-            solved[s, :width, :], solved[s, :width, :], NT, preferred_element_type=jnp.float32
-        )
-        part = weights[owner[s]] * part
-        gram[...] = part if s == 0 else gram[...] + part
+        half = width // 2
+        for low, high in ((0, half), (half, width)):
+            part = lax.dot_general(
+                solved[s, low:high, :],
+                solved[s, low:width, :],
+                NT,
+                preferred_element_type=jnp.float32,
+            )
+            part = weights[owner[s]] * part
+            gram[low:high, low:] = part if s == 0 else gram[low:high, low:] + part
+        if s == count - 1:
+            gram[half:, :half] = gram[:half, half:].T
 
     def times_gram(row):
         part = gram[:, :LANES] * row[:, :LANES]

time: 41.4 us -> 40.5 us (0.978)
  Pallas kernels: 40.6 us -> 39.7 us
    pallas_call x1, Pallas kernels: 40 us -> 39.1 us  [body(): pl.pallas_call(functools.partial(kernel, sizes), out_shape=tuple((pltpu.V...]
where the time goes in v4:
time: 40.5 us; the launch traced here: 40.4 us
  Pallas kernels  39.7 us (98%)
  between operations  0.64 us (2%)
    pallas_call x1, Pallas kernels, body(): pl.pallas_call(functools.partial(kernel, sizes), out_shape=tuple((pltpu.V...  39.1 us

profile of v4, /device:TPU:0, one launch (start us, length us, event | category | flops | bytes accessed | tf_op | source)
XLA Modules:
  0.0 40.4 jit_solution(2200392308453007576)
XLA Ops:
  0.6 39.1 %shard_map.95 = (f32[1,512]{1,0:T(1,128)S(1)}, f32[2,2048]{1,0:T(2,128)S(1)}) custom-call(s32[2]{0:T(128)} %active_ref.1, s32[2]{0:T(128)} %owner_ref.1, f32[64]{0:T(128)} %weights_ref.1, bf16[2,2048]{1,0:T(2,128)(2,1)} %residual_ref.1, f32[1,512]{1,0:T(1,128)} %bitcast.3, f32[1,512]{1,0:T(1,128)} %bitcast.4, bf16[2,2048,2048]{2,1,0:T(8,128)(2,1)} %linv_hbm.1, ...), custom_call_target="tpu_custom_call" | custom-call | tf_op jit(solution)/shard_map/pallas_call | solution.py:302
  39.8 0.6 %shard_map.96 = (f32[1,512]{1,0:T(1,128)}, f32[2,2048]{1,0:T(2,128)}) custom-call(f32[1,512]{1,0:T(1,128)S(1)} %get-tuple-element.6.step_ref, f32[2,2048]{1,0:T(2,128)S(1)} %get-tuple-element.7.newton_ref), custom_call_target="tpu_custom_call" | custom-call | tf_op jit(solution)/shard_map/pallas_call | solution.py:340
